TPU v7x, 32 devices: a whole 2x2x4 slice. The times are simulated.
32 devices in a mesh: groups: 2 (over y), ep: 8 (over z, x), tp: 2 (over core).
Axes of the slice: x: 2, y: 2, z: 4, core: 2. Of those that a mesh axis runs over, the one named last changes fastest.
Arguments:
- residual: bfloat16 [256, 1440], P(('groups', 'ep')), parts along dimension 0, may hold values from -6 to 6
- queries: bfloat16 [256, 2048], P(('groups', 'ep'), 'tp'), parts along dimension 0, may hold values from -7 to 7
- new_kv: bfloat16 [256, 2, 512], P(('groups', 'ep'), None, 'tp'), parts along dimension 0, may hold values from -6 to 6
- kv_cache: bfloat16 [256, 2, 8, 64, 256], P(('groups', 'ep'), None, 'tp'), parts along dimension 0, may hold values from -7 to 7
- cache_len: int32 [256], P(('groups', 'ep')), parts along dimension 0, may hold values from 2 to 255, as said below
- move_slot: int32 [32], P(('groups', 'ep')), parts along dimension 0, may hold values from 0 to 15, as said below
- move_dest: int32 [32], P(('groups', 'ep')), parts along dimension 0, may hold values from 0 to 7, as said below
- sink_logits: float32 [32], P('tp'), may hold values from -1 to 3
- out_weight: bfloat16 [2048, 1440], P('tp'), may hold values from -0.125 to 0.125
- norm_gain: float32 [1440], replicated, may hold values from 0.1 to 1.9
- router_weight: bfloat16 [1440, 8], replicated, may hold values from -0.3125 to 0.3125
- expert_ids: int32 [256, 4], P(('groups', 'ep')), parts along dimension 0, may hold values from 0 to 7, all different within a row; in each aligned block of 16 rows (0 to 15, 16 to 31, ...) at most 16 rows name the same one
- gate_up: bfloat16 [8, 1440, 2, 1440], P('ep', None, None, 'tp'), may hold values from -0.15625 to 0.15625
- down_weight: bfloat16 [8, 1440, 1440], P('ep', 'tp'), may hold values from -0.15625 to 0.15625
Outputs:
- layer_out: bfloat16 [256, 1440], P(('groups', 'ep'), 'tp'), parts along dimension 0
- cache_out: bfloat16 [256, 2, 8, 64, 256], P(('groups', 'ep'), None, 'tp'), parts along dimension 0
There are 2 independent parts, one for each index of `groups`. A program takes and returns all parts, laid end to end along the dimension named above; an argument that names none is the same for every part. Nothing has to cross between parts.
Inputs may be any that keep to these rules, and one draw needn't show every extreme that they name: `cache_len`: values at most 255, which some row reaches. `move_slot`: the 2 entries of one shard are distinct local rows: those of its rows with the largest cache_len. `move_dest`: for each j, the destinations of entry j over all shards form a permutation of the shards (a shard may keep its row). `expert_ids`: each row names 4 different experts; among the 16 rows of one ep index (new placement) no expert is named by more than 16 rows, a bound that some block reaches.
All inputs are finite; a program needn't handle non-finite values.
Results may differ from a plain program's by a relative error of at most 0.0056.
Values may be sent and summed in bfloat16 or wider, within the bound.
A program may use at most 64 MiB of HBM per device.

v0:
```python
import jax
import jax.numpy as jnp
from jax import lax
from jax.sharding import PartitionSpec as P

ALPHA = 1.702
EPSILON = 1e-05


def insert_token(cache_values, new_rows, lengths):
    row_count = cache_values.shape[0]
    kv_count = cache_values.shape[2]
    head_dim = cache_values.shape[3]
    length = cache_values.shape[4]
    fresh_rows = new_rows.reshape(row_count, 2, kv_count, head_dim, 1)
    position_index = lax.broadcasted_iota(jnp.int32, (row_count, 1, 1, 1, length), 4)
    return jnp.where(
        position_index == lengths.reshape(row_count, 1, 1, 1, 1), fresh_rows, cache_values
    )


def attend_rows(queries, cache_values, lengths, sink_logits):
    row_count = cache_values.shape[0]
    kv_count = cache_values.shape[2]
    head_dim = cache_values.shape[3]
    length = cache_values.shape[4]
    group = queries.shape[1] // (kv_count * head_dim)
    query_rows = queries.reshape(row_count, kv_count, group, head_dim)
    scores = jnp.einsum(
        "rgqd,rgdl->rgql", query_rows, cache_values[:, 0], preferred_element_type=jnp.float32
    ) * head_dim ** (-0.5)
    visible = lax.broadcasted_iota(jnp.int32, (row_count, 1, 1, length), 3) <= lengths.reshape(
        row_count, 1, 1, 1
    )
    sink_part = sink_logits.reshape(1, kv_count, group, 1)
    peak_score = jnp.maximum(
        jnp.max(jnp.where(visible, scores, -1e30), axis=3, keepdims=True), sink_part
    )
    weights = jnp.where(visible, jnp.exp(scores - peak_score), 0.0)
    total_mass = jnp.sum(weights, axis=3, keepdims=True) + jnp.exp(sink_part - peak_score)
    probabilities = (weights / total_mass).astype(jnp.bfloat16)
    mixture = jnp.einsum(
        "rgql,rgdl->rgqd", probabilities, cache_values[:, 1], preferred_element_type=jnp.float32
    )
    return mixture.astype(jnp.bfloat16).reshape(row_count, -1)


def migrate(cache_values, residual, queries, lengths, move_slot, move_dest):
    my_shard = lax.axis_index("ep")
    row_count = residual.shape[0]
    move_count = move_slot.shape[0]
    current = (cache_values, residual, queries, lengths)
    leaving = tuple((jnp.take(member, move_slot, axis=0) for member in current))
    piece = (
        lax.all_gather(leaving[0], "ep", axis=0, tiled=True),
        lax.all_gather(leaving[1], "ep", axis=0, tiled=True),
        lax.all_gather(leaving[2], "ep", axis=0, tiled=True),
        lax.all_gather(leaving[3], "ep", axis=0, tiled=True),
        lax.all_gather(move_dest, "ep", axis=0, tiled=True),
    )
    piece_rows = piece[4].shape[0]
    column = jnp.arange(piece_rows, dtype=jnp.int32) % move_count
    target = jnp.where(piece[4] == my_shard, move_slot[column], row_count)
    return tuple(
        (held.at[target].set(incoming, mode="drop") for held, incoming in zip(current, piece[:4]))
    )


def per_device(
    residual,
    queries,
    new_kv,
    kv_cache,
    cache_len,
    move_slot,
    move_dest,
    sink_logits,
    out_weight,
    norm_gain,
    router_weight,
    expert_ids,
    gate_up,
    down_weight,
):
    row_count = residual.shape[0]
    filled = insert_token(kv_cache, new_kv, cache_len)
    cache_new, resid_new, query_new, length_new = migrate(
        filled, residual, queries, cache_len, move_slot, move_dest
    )
    heads = attend_rows(query_new, cache_new, length_new, sink_logits)
    partial_out = jnp.dot(heads, out_weight, preferred_element_type=jnp.float32)
    stream = resid_new.astype(jnp.float32) + lax.psum(partial_out, "tp")
    mean_square = jnp.mean(stream * stream, axis=1, keepdims=True)
    normed = stream * lax.rsqrt(mean_square + EPSILON) * norm_gain
    tokens = normed.astype(jnp.bfloat16)
    logits = jnp.dot(normed, router_weight.astype(jnp.float32), precision=lax.Precision.HIGHEST)
    raised = jnp.exp(jnp.take_along_axis(logits, expert_ids, axis=1))
    gate_weights = raised / jnp.sum(raised, axis=1, keepdims=True)
    top_count = expert_ids.shape[1]
    expert_count = router_weight.shape[1]
    width = tokens.shape[1]
    capacity = max(2, min(row_count, 2 * row_count * top_count // expert_count))
    flat_ids = expert_ids.reshape(-1)
    onehot = (flat_ids[:, None] == jnp.arange(expert_count, dtype=jnp.int32)[None, :]).astype(
        jnp.int32
    )
    slot_rank = jnp.sum((jnp.cumsum(onehot, axis=0) - 1) * onehot, axis=1)
    position = flat_ids * capacity + slot_rank
    owner_row = jnp.arange(row_count * top_count, dtype=jnp.int32) // top_count
    outgoing = (
        jnp.zeros((expert_count * capacity, width), jnp.bfloat16)
        .at[position]
        .set(tokens[owner_row])
    )
    outgoing = outgoing.reshape(expert_count, capacity, width)
    local_experts = gate_up.shape[0]
    share_width = width // lax.axis_size("tp")
    offset = lax.axis_index("tp") * share_width
    features = lax.all_to_all(outgoing, "ep", split_axis=0, concat_axis=0, tiled=True)
    slot_count = features.shape[1]
    grouped = features.reshape(-1, local_experts, slot_count, features.shape[2])
    gate_and_up = jnp.einsum(
        "secd,edkf->seckf", grouped, gate_up, preferred_element_type=jnp.float32
    )
    gate_part = gate_and_up[:, :, :, 0, :]
    up_part = gate_and_up[:, :, :, 1, :]
    hidden = ((up_part + 1.0) * gate_part * jax.nn.sigmoid(ALPHA * gate_part)).astype(jnp.bfloat16)
    partial_down = jnp.einsum(
        "secf,efd->secd", hidden, down_weight, preferred_element_type=jnp.float32
    )
    summed = lax.psum_scatter(
        partial_down.reshape(-1, slot_count, partial_down.shape[3]),
        "tp",
        scatter_dimension=2,
        tiled=True,
    )
    returned = lax.all_to_all(
        summed.astype(jnp.bfloat16), "ep", split_axis=0, concat_axis=0, tiled=True
    )
    back_rows = returned.reshape(expert_count * capacity, -1)[position].astype(jnp.float32)
    mixture = jnp.sum(
        back_rows.reshape(row_count, top_count, -1) * gate_weights[:, :, None], axis=1
    )
    own_stream = lax.dynamic_slice_in_dim(stream, offset, share_width, 1)
    layer_out = (own_stream + mixture).astype(jnp.bfloat16)
    return (layer_out, cache_new)


def solution(mesh):
    in_specs = (
        P(("groups", "ep"), None),
        P(("groups", "ep"), "tp"),
        P(("groups", "ep"), None, "tp"),
        P(("groups", "ep"), None, "tp", None, None),
        P(("groups", "ep")),
        P(("groups", "ep")),
        P(("groups", "ep")),
        P("tp"),
        P("tp", None),
        P(),
        P(),
        P(("groups", "ep"), None),
        P("ep", None, None, "tp"),
        P("ep", "tp", None),
    )
    out_specs = (P(("groups", "ep"), "tp"), P(("groups", "ep"), None, "tp", None, None))
    return jax.shard_map(
        per_device, mesh=mesh, in_specs=in_specs, out_specs=out_specs, check_vma=False
    )
```

profile of v0, /device:TPU:1, one launch (start us, length us, event | category | flops | bytes accessed | tf_op | source)
XLA Modules:
  0.0 203.4 jit_solution(2300764731975004096)
XLA Ops:
  11.9 4.2 %broadcast_select_fusion = bf16[16,2,4,64,256]{4,3,2,1,0:T(8,128)(2,1)} fusion(bf16[16,2,4,64,256]{4,3,2,1,0:T(8,128)(2,1)} %param.17, pred[16,256]{1,0:T(8,128)(4,1)S(1)} %iota_compare_fusion.1, bf16[16,2,4,64]{3,2,1,0:T(4,128)(2,1)S(1)} %broadcast_in_dim.107), kind=kLoop, calls=%fused_computation.15 | loop fusion | flops 2097152 | bytes 8409088 | tf_op jit(solution)/shard_map/jit(_where)/select_n | solution.py:17
  16.1 3.6 %gather_fusion.3 = bf16[2,2,4,64,256]{4,3,2,1,0:T(8,128)(2,1)} fusion(bf16[16,2,4,64,256]{4,3,2,1,0:T(8,128)(2,1)} %broadcast_select_fusion, s32[1024]{0:T(1024)S(1)} %pad_clamp_fusion.2), kind=kCustom, calls=%fused_computation.3 | custom fusion | bytes 1048584 | tf_op jit(solution)/shard_map/jit(_take)/gather | solution.py:53
  21.0 1.9 broadcast_select_fusion.1
  23.3 9.5 %all-reduce.2 = (s32[16]{0:T(128)S(1)}, s32[16]{0:T(128)S(1)}) all-reduce(s32[16]{0:T(128)S(1)} %dynamic-update-slice, s32[16]{0:T(128)S(1)} %get-tuple-element.8), channel_id=1, replica_groups=mesh['groups'=2,'ep'=8,'tp'=2] {'ep'}, use_global_device_ids=true, to_apply=%add | all-reduce | flops 32 | bytes 256
  33.5 24.5 %all-gather.1 = bf16[8,2,1024]{2,1,0:T(2,128)(2,1)S(1)} all-gather(bf16[1,2,1024]{2,1,0:T(2,128)(2,1)S(1)} %fusion.33), channel_id=1, replica_groups=mesh['groups'=2,'ep'=8,'tp'=2] {'ep'}, dimensions={0}, use_global_device_ids=true | all-gather | bytes 36864 | tf_op jit(solution)/shard_map/all_gather | solution.py:57
  58.6 1.2 compare_select_fusion.4
  62.0 24.7 %all-gather = bf16[8,2,1440]{2,1,0:T(2,128)(2,1)S(1)} all-gather(bf16[1,2,1440]{2,1,0:T(2,128)(2,1)S(1)} %fusion.32), channel_id=1, replica_groups=mesh['groups'=2,'ep'=8,'tp'=2] {'ep'}, dimensions={0}, use_global_device_ids=true | all-gather | bytes 51840 | tf_op jit(solution)/shard_map/all_gather | solution.py:56
  88.2 10.6 %all-gather.4.cloned.1.call-done = bf16[16,2,4,64,256]{4,3,2,1,0:T(8,128)(2,1)} async-done(((bf16[2,2,4,64,256]{4,3,2,1,0:T(8,128)(2,1)}), bf16[16,2,4,64,256]{4,3,2,1,0:T(8,128)(2,1)}) %all-gather.4.cloned.1.call-update) | async-done | bytes 4194320 | tf_op jit(solution)/shard_map/all_gather | solution.py:55
  98.8 8.6 %scatter_fusion.3 = bf16[16,2,4,64,256]{4,3,2,1,0:T(8,128)(2,1)} fusion(bf16[16,2,4,64,256]{4,3,2,1,0:T(8,128)(2,1)} %broadcast_select_fusion, s32[16]{0:T(128)S(1)} %compare_select_fusion.4, bf16[16,2,4,64,256]{4,3,2,1,0:T(8,128)(2,1)} %all-gather.4.cloned.1.call-done), kind=kCustom, calls=%fused_computation.10 | custom fusion | bytes 12582976 | tf_op jit(solution)/shard_map/scatter | solution.py:65
  107.4 2.1 %select_reduce_fusion = (f32[16,4,4]{2,1,0:T(4,128)S(1)}, f32[16,4,4,256]{3,2,1,0:T(4,128)S(1)}) fusion(pred[16,256]{1,0:T(8,128)(4,1)S(1)} %iota_compare_fusion.2, bf16[16,4,4,64]{3,2,1,0:T(4,128)(2,1)S(1)} %reshape.249, bf16[16,2,4,64,256]{4,3,2,1,0:T(8,128)(2,1)} %scatter_fusion.3), kind=kOutput, calls=%fused_computation.32 | convolution fusion | flops 8584960 | bytes 2397184 | tf_op jit(solution)/shard_map/rgqd,rgdl->rgql/dot_general | solution.py:29
  109.9 2.3 %fusion.11 = bf16[16,4,4,64]{3,2,1,0:T(4,128)(2,1)S(1)} fusion(bf16[16,2,4,64,256]{4,3,2,1,0:T(8,128)(2,1)} %scatter_fusion.3, f32[16,4,4,256]{3,2,1,0:T(4,128)S(1)} %get-tuple-element.13, f32[16,4,4]{2,1,0:T(4,128)S(1)} %bitcast.87, f32[16,4,4]{2,1,0:T(4,128)S(1)} %bitcast.86, pred[16,256]{1,0:T(8,128)(4,1)S(1)} %iota_compare_fusion.2), kind=kOutput, calls=%fused_computation.24 | convolution fusion | flops 8667136 | bytes 2398208 | tf_op jit(solution)/shard_map/rgql,rgdl->rgqd/dot_general | solution.py:42
  112.3 1.5 fusion.42
  114.0 21.1 %all-reduce.5.cloned.1.call-done = f32[16,1440]{1,0:T(8,128)} async-done(((f32[16,1440]{1,0:T(8,128)}), f32[16,1440]{1,0:T(8,128)}) %all-reduce.5.cloned.1.call-update) | async-done | bytes 92176 | tf_op jit(solution)/shard_map/psum | solution.py:92
  136.1 1.7 scatter_custom_fusion.4
  137.8 16.7 %all_to_all.10 = bf16[8,16,1440]{2,1,0:T(8,128)(2,1)S(1)} all-to-all(bf16[8,16,1440]{2,1,0:T(8,128)(2,1)S(1)} %bitcast.81), channel_id=1, replica_groups=mesh['groups'=2,'ep'=8,'tp'=2] {'ep'}, dimensions={0} | all-to-all | bytes 737280 | tf_op jit(solution)/shard_map/all_to_all | solution.py:119
  154.5 3.2 %fusion.7 = f32[8,1,16,2,720]{4,2,3,0,1:T(8,128)S(1)} fusion(bf16[1440,2,720]{2,1,0:T(2,128)(2,1)} %bitcast.90, bf16[8,16,1440]{2,1,0:T(8,128)(2,1)S(1)} %all_to_all.10), kind=kOutput, calls=%fused_computation.22 | convolution fusion | flops 530841600 | bytes 5253120 | tf_op jit(solution)/shard_map/secd,edkf->seckf/dot_general | solution.py:122
  157.7 1.4 fusion.3
  159.1 4.8 %copy.48 = f32[8,16,1440]{1,0,2:T(8,128)} copy(f32[8,16,1440]{2,1,0:T(8,128)} %fusion.3) | data formatting | bytes 1474560
  163.9 5.0 %reshape.397 = f32[1440,128]{1,0:T(8,128)} reshape(f32[1440,8,16]{2,1,0:T(8,128)} %bitcast.78) | data formatting | bytes 1474560
  170.3 7.0 %reduce-scatter.4.cloned.1.call-done = f32[720,128]{1,0:T(8,128)} async-done(((f32[1440,128]{1,0:T(8,128)}), f32[720,128]{1,0:T(8,128)}) %reduce-scatter.4.cloned.1.call-update) | async-done | bytes 368656
  177.3 2.8 %reshape.398 = bf16[720,8,16]{2,1,0:T(8,128)(2,1)} reshape(f32[720,128]{1,0:T(8,128)} %reduce-scatter.4.cloned.1.call-done) | data formatting | bytes 552960
  180.1 2.5 %copy.49 = bf16[8,16,720]{2,1,0:T(8,128)(2,1)} copy(bf16[8,16,720]{1,0,2:T(8,128)(2,1)} %bitcast.79) | data formatting | bytes 368640
  182.6 5.6 %all-to-all-start.1 = ((bf16[8,16,720]{2,1,0:T(8,128)(2,1)}), bf16[8,16,720]{2,1,0:T(8,128)(2,1)S(1)}, u32[]{:S(2)}, u32[]{:S(2)}) async-start(bf16[8,16,720]{2,1,0:T(8,128)(2,1)} %copy.49), calls=%async_computation.1 | async-start | bytes 393216 | tf_op jit(solution)/shard_map/all_to_all | solution.py:137
  188.4 6.8 %all-to-all-done.1 = bf16[8,16,720]{2,1,0:T(8,128)(2,1)S(1)} async-done(((bf16[8,16,720]{2,1,0:T(8,128)(2,1)}), bf16[8,16,720]{2,1,0:T(8,128)(2,1)S(1)}, u32[]{:S(2)}, u32[]{:S(2)}) %all-to-all-start.1) | async-done | bytes 184352 | tf_op jit(solution)/shard_map/all_to_all | solution.py:137
  (85 shorter events, 15.4 us)
Async XLA Ops:
  7.2 105.2 %copy-start = (bf16[1024,1440]{0,1:T(8,128)(2,1)S(1)}, bf16[1024,1440]{0,1:T(8,128)(2,1)}, u32[]{:S(2)}) copy-start(bf16[1024,1440]{0,1:T(8,128)(2,1)} %param.22) | copy-start | bytes 8847364
  7.2 91.7 %all-gather.4.cloned.1.call-start = ((), (), s32[]{:S(2)}) async-start(), calls=%async_computation.3 | async-start | bytes 4718592 | tf_op jit(solution)/shard_map/all_gather | solution.py:55
  11.8 7.9 %copy-start.8 = (u32[32]{0:T(128)S(1)}, u32[32]{0:T(128)}, u32[]{:S(2)}) copy-start(u32[32]{0:T(128)} %constant.165) | copy-start | bytes 388
  11.8 9.1 %copy-start.4 = (s32[2]{0:T(128)S(1)}, s32[2]{0:T(128)}, u32[]{:S(2)}) copy-start(s32[2]{0:T(128)} %param.19) | copy-start | bytes 28
  11.8 11.2 %copy-start.7 = (s32[2]{0:T(128)S(1)}, s32[2]{0:T(128)}, u32[]{:S(2)}) copy-start(s32[2]{0:T(128)} %param.20) | copy-start | bytes 28
  16.1 45.2 %copy-start.5 = (f32[16]{0:T(128)S(1)}, f32[16]{0:T(128)}, u32[]{:S(2)}) copy-start(f32[16]{0:T(128)} %param.21) | copy-start | bytes 196
  16.1 71.3 %copy-start.3 = (s32[16,4]{0,1:T(4,128)S(1)}, s32[16,4]{0,1:T(4,128)}, u32[]{:S(2)}) copy-start(s32[16,4]{0,1:T(4,128)} %param.25) | copy-start | bytes 772
  23.0 112.0 %all-reduce.5.cloned.1.call-start = ((), (), s32[]{:S(2)}) async-start(), calls=%async_computation.4 | async-start | bytes 196608 | tf_op jit(solution)/shard_map/psum | solution.py:92
  109.9 26.2 %copy-start.1 = (f32[1440]{0:T(1024)S(1)}, f32[1440]{0:T(1024)}, u32[]{:S(2)}) copy-start(f32[1440]{0:T(1024)} %param.23) | copy-start | bytes 17284
  113.9 63.4 %reduce-scatter.4.cloned.1.call-start = ((), (), s32[]{:S(2)}) async-start(), calls=%async_computation.5 | async-start | bytes 1105920
  154.5 3.2 %copy-start.6 = (bf16[1,720,1440]{2,1,0:T(8,128)(2,1)S(1)}, bf16[1,720,1440]{2,1,0:T(8,128)(2,1)}, u32[]{:S(2)}) copy-start(bf16[1,720,1440]{2,1,0:T(8,128)(2,1)} %param.27) | copy-start | bytes 6220804
  163.9 5.3 %copy-start.2 = (bf16[1440,8]{0,1:T(8,128)(2,1)S(1)}, bf16[1440,8]{0,1:T(8,128)(2,1)}, u32[]{:S(2)}) copy-start(bf16[1440,8]{0,1:T(8,128)(2,1)} %param.24) | copy-start | bytes 69124
  182.6 12.6 %all-to-all-start.1 = ((bf16[8,16,720]{2,1,0:T(8,128)(2,1)}), bf16[8,16,720]{2,1,0:T(8,128)(2,1)S(1)}, u32[]{:S(2)}, u32[]{:S(2)}) async-start(bf16[8,16,720]{2,1,0:T(8,128)(2,1)} %copy.49), calls=%async_computation.1 | async-start | bytes 393216 | tf_op jit(solution)/shard_map/all_to_all | solution.py:137
Sparse Core Ops, SparseCore 0:
  23.1 75.6 all-gather.3
  114.0 20.9 all-reduce.4
  169.0 8.2 reduce-scatter.3
where the time goes:
time: 206 us; the launch traced here: 203 us
  blocking collectives  75.3 us (37%)
  waiting for transfers between devices  45.5 us (22%)
  local copies, waits for them, and re-layouts  40 us (19%)
  between operations  14.7 us (7%)
  other arithmetic  11.3 us (5%)
  matrix products  10.7 us (5%)
  starting transfers between devices  5.73 us (3%)
    all_gather x1, blocking collectives, migrate(): lax.all_gather(leaving[1], 'ep', axis=0, tiled=True)  24.7 us
    all_gather x1, blocking collectives, migrate(): lax.all_gather(leaving[2], 'ep', axis=0, tiled=True)  24.5 us
    psum x1, waiting for transfers between devices, per_device(): stream = resid_new.astype(jnp.float32) + lax.psum(partial_out, 'tp')  21.1 us
    unnamed x34, local copies, waits for them, and re-layouts  18.5 us
    all_to_all x1, blocking collectives, per_device(): lax.all_to_all(outgoing, 'ep', split_axis=0, concat_axis=0, tiled=True)  16.7 us
    scatter x4, local copies, waits for them, and re-layouts, migrate(): held.at[target].set(incoming, mode='drop')  10.6 us
    all_gather x1, waiting for transfers between devices, migrate(): lax.all_gather(leaving[0], 'ep', axis=0, tiled=True)  10.6 us
    unnamed x1, blocking collectives  9.55 us
  transfers between devices with their start and end apart: 4, of which 4 were waited for; matrix products, arithmetic and copies ran while one was open for 4% of the time, Pallas kernels for 0%

commit v1 on v0

--- a/solution.py
+++ b/solution.py
@@ -1,6 +1,10 @@
+import functools
+
 import jax
 import jax.numpy as jnp
 from jax import lax
+from jax.experimental import pallas as pl
+from jax.experimental.pallas import tpu as pltpu
 from jax.sharding import PartitionSpec as P
 
 ALPHA = 1.702
@@ -66,7 +70,7 @@
     )
 
 
-def per_device(
+def per_device_general(
     residual,
     queries,
     new_kv,
@@ -146,7 +150,385 @@
     return (layer_out, cache_new)
 
 
+MESH = pl.DeviceIdType.MESH
+F32 = jnp.float32
+BF16 = jnp.bfloat16
+
+
+def wrap(value, size):
+    value = jnp.where(value < 0, value + size, value)
+    return jnp.where(value >= size, value - size, value)
+
+
+def step_kernel(
+    n_ep,
+    n_tp,
+    lengths,
+    slots,
+    meta,
+    queries,
+    residual,
+    sink,
+    gain,
+    router,
+    expert_ids,
+    cache_hbm,
+    out_hbm,
+    gate_up_hbm,
+    down_hbm,
+    layer_out,
+    incoming,
+    cache,
+    out_w,
+    gate_up,
+    down_w,
+    send1,
+    recv1,
+    send2,
+    recv2,
+    meta_all,
+    meta_smem,
+    mixed,
+    heads,
+    partial,
+    partial_in,
+    own_stream,
+    streams,
+    hidden,
+    ysend,
+    yrecv,
+    local_sem,
+    meta_sems,
+    one_sems,
+    two_sems,
+    part_sems,
+    stream_sems,
+    y_sems,
+    in_sem,
+):
+    ep = lax.axis_index("ep")
+    tp = lax.axis_index("tp")
+    rows, q_heads, lanes = mixed.shape
+    width = residual.shape[1]
+    half = width // n_tp
+    pieces = cache.shape[1]
+    kv = pieces // 2
+    hd = cache.shape[2]
+    moves = send1.shape[1]
+    group = q_heads // kv
+
+    def ahead(k):
+        return lax.rem(ep + k, n_ep)
+
+    def behind(k):
+        return lax.rem(ep - k + n_ep, n_ep)
+
+    loads = [
+        pltpu.make_async_copy(cache_hbm, cache, local_sem.at[0]),
+        pltpu.make_async_copy(out_hbm, out_w, local_sem.at[1]),
+        pltpu.make_async_copy(gate_up_hbm, gate_up, local_sem.at[2]),
+        pltpu.make_async_copy(down_hbm, down_w, local_sem.at[3]),
+    ]
+    for load in loads:
+        load.start()
+
+    barrier = pltpu.get_barrier_semaphore()
+    for k in range(n_ep):
+        for q in range(n_tp):
+            if k or q:
+                pl.semaphore_signal(
+                    barrier,
+                    inc=1,
+                    device_id={"ep": ahead(k), "tp": lax.rem(tp + q, n_tp)},
+                    device_id_type=MESH,
+                )
+    pl.semaphore_wait(barrier, n_ep * n_tp - 1)
+
+    def send(src, dst, sems, index, k, q=0):
+        target = {"ep": ahead(k)} if k else {}
+        if q:
+            target["tp"] = lax.rem(tp + q, n_tp)
+        copy = pltpu.make_async_remote_copy(
+            src_ref=src,
+            dst_ref=dst,
+            send_sem=sems.at[(0,) + index],
+            recv_sem=sems.at[(1,) + index],
+            device_id=target,
+            device_id_type=MESH,
+        )
+        copy.start()
+        return copy
+
+    meta_copies = [send(meta, meta_all.at[k], meta_sems, (k,), k) for k in range(1, n_ep)]
+    meta_all[0] = meta[...]
+
+    loads[0].wait()
+    for j in range(moves):
+        slot = slots[j]
+        for p in range(pieces):
+            send1[p, j] = cache[slot, p]
+    one_copies = [
+        send(send1.at[ahead(k)], recv1.at[k], one_sems, (k,), k) for k in range(1, n_ep)
+    ]
+    recv1[0] = send1[ep]
+
+    position_index = lax.broadcasted_iota(jnp.int32, (q_heads, cache.shape[3]), 1)
+    sink_part = sink[...]
+
+    def attend(r, carry):
+        keys = cache[r, 0:kv].reshape(kv * hd, cache.shape[3])
+        values = cache[r, kv : 2 * kv].reshape(kv * hd, cache.shape[3])
+        scores = jnp.dot(queries[r], keys, preferred_element_type=F32) * hd ** (-0.5)
+        visible = position_index <= lengths[r]
+        peak = jnp.maximum(
+            jnp.max(jnp.where(visible, scores, -1e30), axis=1, keepdims=True), sink_part
+        )
+        weights = jnp.where(visible, jnp.exp(scores - peak), 0.0)
+        mass = jnp.sum(weights, axis=1, keepdims=True) + jnp.exp(sink_part - peak)
+        probs = (weights / mass).astype(BF16)
+        mixed[r] = lax.dot_general(
+            probs, values, (((1,), (1,)), ((), ())), preferred_element_type=F32
+        )
+        return carry
+
+    lax.fori_loop(0, rows, attend, 0, unroll=4)
+    for h in range(0, q_heads, 2):
+        g = h // group
+        pair = [mixed[:, h + i, g * hd : (g + 1) * hd] for i in range(2)]
+        heads[:, h * hd : (h + 2) * hd] = jnp.concatenate(pair, axis=1).astype(BF16)
+
+    loads[1].wait()
+    partial[...] = lax.dot_general(
+        heads[...], out_w[...], (((1,), (1,)), ((), ())), preferred_element_type=F32
+    )
+    part_copies = [send(partial, partial_in.at[q], part_sems, (q,), 0, q) for q in range(1, n_tp)]
+    total = partial[...]
+    for q in range(1, n_tp):
+        part_copies[q - 1].wait()
+        total = total + partial_in[q]
+    stream = residual[...].astype(F32) + total
+    own_stream[...] = stream
+    streams[0] = stream.astype(BF16)
+    stream_copies = [
+        send(streams.at[0], streams.at[k], stream_sems, (k,), k) for k in range(1, n_ep)
+    ]
+
+    for copy in meta_copies:
+        copy.wait()
+    to_smem = pltpu.make_async_copy(meta_all, meta_smem, in_sem)
+    to_smem.start()
+    to_smem.wait()
+    slot_of = [[meta_smem[k, 0, j] for j in range(moves)] for k in range(n_ep)]
+    dest_of = [[meta_smem[k, 0, moves + j] for j in range(moves)] for k in range(n_ep)]
+
+    all_rows = n_ep * rows
+    new_index = lax.broadcasted_iota(jnp.int32, (all_rows, all_rows), 0)
+    old_index = lax.broadcasted_iota(jnp.int32, (all_rows, all_rows), 1)
+    home = jnp.where(new_index < rows, new_index, 0)
+    for k in range(1, n_ep):
+        inside = (new_index >= k * rows) & (new_index < (k + 1) * rows)
+        home = jnp.where(inside, new_index + (n_ep - 2 * k) * rows, home)
+    source_of = [[None] * moves for _ in range(n_ep)]
+    for k in range(n_ep):
+        shard = ahead(k)
+        receiver = (n_ep - k) % n_ep
+        for j in range(moves):
+            found = jnp.int32(0)
+            leaving = jnp.int32(0)
+            for s in range(n_ep):
+                hit = dest_of[s][j] == shard
+                found = jnp.where(hit, s, found)
+                leaving = jnp.where(hit, s * rows + slot_of[s][j], leaving)
+            source_of[k][j] = found
+            home = jnp.where(new_index == k * rows + slot_of[receiver][j], leaving, home)
+    move_to = jnp.where(old_index == home, 1.0, 0.0).astype(BF16)
+
+    for copy in one_copies:
+        copy.wait()
+    for k in range(n_ep):
+        for j in range(moves):
+            send2[k, j] = recv1[source_of[k][j], j]
+    for copy in stream_copies:
+        copy.wait()
+    two_copies = [send(send2.at[k], recv2.at[k], two_sems, (k,), k) for k in range(1, n_ep)]
+    recv2[0] = send2[0]
+
+    known = streams[...].reshape(all_rows, width)
+    wide = known.astype(F32)
+    mean_square = jnp.sum(wide * wide, axis=1, keepdims=True) * (1.0 / width)
+    tokens = (wide * lax.rsqrt(mean_square + EPSILON) * gain[...]).astype(BF16)
+    loads[2].wait()
+    gate_part = jnp.dot(tokens, gate_up[:, 0, :], preferred_element_type=F32)
+    up_part = jnp.dot(tokens, gate_up[:, 1, :], preferred_element_type=F32)
+    hidden[...] = ((up_part + 1.0) * gate_part * jax.nn.sigmoid(ALPHA * gate_part)).astype(BF16)
+    moved = jnp.dot(move_to, hidden[...], preferred_element_type=F32).astype(BF16)
+    loads[3].wait()
+    expert_out = jnp.dot(moved, down_w[...], preferred_element_type=F32)
+    for c in range(n_tp):
+        ysend[c] = (
+            expert_out[:, c * half : (c + 1) * half].astype(BF16).reshape(n_ep, rows, half)
+        )
+    y_copies = []
+    for q in range(n_tp):
+        core = lax.rem(tp + q, n_tp)
+        for k in range(n_ep):
+            if k or q:
+                y_copies.append(send(ysend.at[core, k], yrecv.at[q, k], y_sems, (q, k), k, q))
+    yrecv[0, 0] = ysend[tp, 0]
+
+    row_index = lax.broadcasted_iota(jnp.int32, (rows, 1), 0)
+    kept = row_index >= 0
+    for j in range(moves):
+        kept = kept & (row_index != slot_of[0][j])
+    brought = jnp.dot(move_to[0:rows], known, preferred_element_type=F32)
+    new_stream = jnp.where(kept, own_stream[...], brought)
+    mean_square = jnp.sum(new_stream * new_stream, axis=1, keepdims=True) * (1.0 / width)
+    normed = new_stream * lax.rsqrt(mean_square + EPSILON) * gain[...]
+    logits = lax.dot_general(
+        normed,
+        router[...].astype(F32),
+        (((1,), (1,)), ((), ())),
+        precision=lax.Precision.HIGHEST,
+        preferred_element_type=F32,
+    )
+    expert_index = lax.broadcasted_iota(jnp.int32, logits.shape, 1)
+    chosen = jnp.zeros(logits.shape, F32)
+    for t in range(expert_ids.shape[1]):
+        chosen = jnp.where(expert_index == expert_ids[:, t : t + 1], 1.0, chosen)
+    best = jnp.max(jnp.where(chosen > 0.5, logits, -1e30), axis=1, keepdims=True)
+    raised = jnp.where(chosen > 0.5, jnp.exp(logits - best), 0.0)
+    gates = raised / jnp.sum(raised, axis=1, keepdims=True)
+    result = new_stream[:, 0:half]
+    for c in range(1, n_tp):
+        result = jnp.where(tp == c, new_stream[:, c * half : (c + 1) * half], result)
+    for copy in y_copies:
+        copy.wait()
+    for k in range(n_ep):
+        gate = jnp.sum(
+            jnp.where(expert_index == behind(k), gates, 0.0), axis=1, keepdims=True
+        )
+        summed = yrecv[0, k].astype(F32)
+        for q in range(1, n_tp):
+            summed = summed + yrecv[q, k].astype(F32)
+        result = result + gate * summed
+    layer_out[...] = result.astype(BF16)
+
+    for copy in two_copies:
+        copy.wait()
+    for k in range(n_ep):
+        for j in range(moves):
+            incoming[j, behind(k)] = recv2[k, j]
+
+
+def per_device(
+    n_ep,
+    n_tp,
+    residual,
+    queries,
+    new_kv,
+    kv_cache,
+    cache_len,
+    move_slot,
+    move_dest,
+    sink_logits,
+    out_weight,
+    norm_gain,
+    router_weight,
+    expert_ids,
+    gate_up,
+    down_weight,
+):
+    rows, width = residual.shape
+    _, _, kv, hd, length = kv_cache.shape
+    moves = move_slot.shape[0]
+    q_heads = sink_logits.shape[0]
+    group = q_heads // kv
+    hidden_units = down_weight.shape[1]
+    filled = insert_token(kv_cache, new_kv, cache_len)
+    pieces = filled.reshape(rows, 2 * kv, hd, length)
+    same = jnp.eye(kv, dtype=queries.dtype).reshape(1, kv, 1, kv, 1)
+    spread = (queries.reshape(rows, kv, group, 1, hd) * same).reshape(rows, q_heads, kv * hd)
+    listing = jnp.concatenate([move_slot, move_dest])
+    meta = jnp.broadcast_to(jnp.pad(listing, (0, 128 - 2 * moves)), (8, 128))
+    piece = (moves, hd, length)
+    half = width // n_tp
+    smem = pl.BlockSpec(memory_space=pltpu.SMEM)
+    vmem = pl.BlockSpec(memory_space=pltpu.VMEM)
+    hbm = pl.BlockSpec(memory_space=pl.ANY)
+    dma = pltpu.SemaphoreType.DMA
+    layer_out, incoming = pl.pallas_call(
+        functools.partial(step_kernel, n_ep, n_tp),
+        out_shape=(
+            jax.ShapeDtypeStruct((rows, half), BF16),
+            jax.ShapeDtypeStruct((moves, 2 * kv, hd, length), BF16),
+        ),
+        in_specs=[smem] * 2 + [vmem] * 7 + [hbm] * 4,
+        out_specs=(vmem, vmem),
+        scratch_shapes=[
+            pltpu.VMEM(pieces.shape, BF16),
+            pltpu.VMEM((width, out_weight.shape[0]), BF16),
+            pltpu.VMEM((width, 2, hidden_units), BF16),
+            pltpu.VMEM((hidden_units, width), BF16),
+            pltpu.VMEM((2 * kv,) + piece, BF16),
+            pltpu.VMEM((n_ep,) + piece, BF16),
+            pltpu.VMEM((n_ep,) + piece, BF16),
+            pltpu.VMEM((n_ep,) + piece, BF16),
+            pltpu.VMEM((n_ep, 8, 128), jnp.int32),
+            pltpu.SMEM((n_ep, 8, 128), jnp.int32),
+            pltpu.VMEM((rows, q_heads, kv * hd), F32),
+            pltpu.VMEM((rows, q_heads * hd), BF16),
+            pltpu.VMEM((rows, width), F32),
+            pltpu.VMEM((n_tp, rows, width), F32),
+            pltpu.VMEM((rows, width), F32),
+            pltpu.VMEM((n_ep, rows, width), BF16),
+            pltpu.VMEM((n_ep * rows, hidden_units), BF16),
+            pltpu.VMEM((n_tp, n_ep, rows, half), BF16),
+            pltpu.VMEM((n_tp, n_ep, rows, half), BF16),
+            dma((4,)),
+            dma((2, n_ep)),
+            dma((2, n_ep)),
+            dma((2, n_ep)),
+            dma((2, n_tp)),
+            dma((2, n_ep)),
+            dma((2, n_tp, n_ep)),
+            dma,
+        ],
+        compiler_params=pltpu.CompilerParams(
+            collective_id=0, has_side_effects=True, vmem_limit_bytes=48 * 1024 * 1024
+        ),
+    )(
+        cache_len,
+        move_slot,
+        meta,
+        spread,
+        residual,
+        sink_logits.reshape(q_heads, 1),
+        norm_gain.reshape(1, width),
+        router_weight.T,
+        expert_ids,
+        pieces,
+        out_weight.T,
+        gate_up[0],
+        down_weight[0],
+    )
+    incoming = incoming.reshape((moves,) + kv_cache.shape[1:])
+    cache_out = filled
+    for j in range(moves):
+        cache_out = lax.dynamic_update_slice(
+            cache_out, incoming[j : j + 1], (move_slot[j], 0, 0, 0, 0)
+        )
+    return layer_out, cache_out
+
+
 def solution(mesh):
+    n_ep, n_tp = mesh.shape["ep"], mesh.shape["tp"]
+
+    def body(*arrays):
+        kv_cache, gate_up = arrays[3], arrays[12]
+        if 2 * kv_cache.shape[2] == n_ep and gate_up.shape[0] == 1 and n_tp == 2:
+            return per_device(n_ep, n_tp, *arrays)
+        return per_device_general(*arrays)
+
     in_specs = (
         P(("groups", "ep"), None),
         P(("groups", "ep"), "tp"),
@@ -165,5 +547,5 @@
     )
     out_specs = (P(("groups", "ep"), "tp"), P(("groups", "ep"), None, "tp", None, None))
     return jax.shard_map(
-        per_device, mesh=mesh, in_specs=in_specs, out_specs=out_specs, check_vma=False
-    )
+        body, mesh=mesh, in_specs=in_specs, out_specs=out_specs, check_vma=False
+    )

time: 206 us -> 69.4 us (0.34); the launches traced: 203 us -> 68.9 us
  blocking collectives: 75.3 us -> 0 us
  Pallas kernels: 0 us -> 50.4 us
  waiting for transfers between devices: 45.5 us -> 0 us
  local copies, waits for them, and re-layouts: 40 us -> 8.06 us
  matrix products: 10.7 us -> 0 us
  between operations: 14.7 us -> 4.62 us
  starting transfers between devices: 5.73 us -> 0 us
  other arithmetic: 11.3 us -> 5.86 us
    pallas_call x0 -> x1, Pallas kernels: none -> 50.4 us  [per_device(): pl.pallas_call(functools.partial(step_kernel, n_ep, n_tp), out_shape=(jax...]
    all_gather x2 -> x0, blocking collectives: 49.1 us -> none  [the longest x1 24.7 us: migrate(): lax.all_gather(leaving[1], 'ep', axis=0, tiled=True)]
    psum x1 -> x0, waiting for transfers between devices: 21.1 us -> none  [per_device(): stream = resid_new.astype(jnp.float32) + lax.psum(partial_out, 'tp')]
    unnamed x34 -> x14, local copies, waits for them, and re-layouts: 18.5 us -> 1.64 us
    all_to_all x1 -> x0, blocking collectives: 16.7 us -> none  [per_device(): lax.all_to_all(outgoing, 'ep', split_axis=0, concat_axis=0, tiled=True)]
    scatter x5 -> x0, local copies, waits for them, and re-layouts: 12.3 us -> none  [the longest x4 10.6 us: migrate(): held.at[target].set(incoming, mode='drop')]
    dot_general x6 -> x0, matrix products: 10.7 us -> none  [the longest x1 3.18 us: per_device(): jnp.einsum('secd,edkf->seckf', grouped, gate_up, preferred_element_type=j...]
    all_gather x1 -> x0, waiting for transfers between devices: 10.6 us -> none  [migrate(): lax.all_gather(leaving[0], 'ep', axis=0, tiled=True)]
  transfers between devices with their start and end apart: 4 -> 0, of which waited for: 4 -> 0; matrix products, arithmetic and copies ran while one was open for 4% -> 0% of each run, Pallas kernels for 0% -> 0%
where the time goes in v1:
time: 69.4 us; the launch traced here: 68.9 us
  Pallas kernels  50.4 us (73%)
  local copies, waits for them, and re-layouts  8.06 us (12%)
  other arithmetic  5.86 us (8%)
  between operations  4.62 us (7%)
    pallas_call x1, Pallas kernels, per_device(): pl.pallas_call(functools.partial(step_kernel, n_ep, n_tp), out_shape=(jax...  50.4 us
    select_n x1, other arithmetic, insert_token(): jnp.where(position_index == lengths.reshape(row_count, 1, 1, 1, 1), fresh...  4.37 us
    unnamed x14, local copies, waits for them, and re-layouts  1.64 us
    dynamic_update_slice x2, local copies, waits for them, and re-layouts, per_device(): lax.dynamic_update_slice(cache_out, incoming[j:j + 1], (move_slot[j], 0,...  1.45 us

profile of v1, /device:TPU:1, one launch (start us, length us, event | category | flops | bytes accessed | tf_op | source)
XLA Modules:
  0.0 68.9 jit_solution(8199653766217760544)
XLA Ops:
  0.6 0.7 %pad_add_fusion = s32[4]{0:T(128)S(1)} fusion(s32[2]{0:T(128)} %param.20, s32[2]{0:T(128)} %slots.1), kind=kLoop, calls=%fused_computation.5 | loop fusion | flops 4 | bytes 32 | tf_op jit(solution)/shard_map/concatenate | solution.py:451
  1.4 1.3 %fusion.2 = (s32[1]{0:T(128)}, s32[1]{0:T(128)}) fusion(s32[2]{0:T(128)} %slots.1), kind=kLoop, calls=%fused_computation.9 | loop fusion | bytes 16 | tf_op jit(solution)/shard_map/slice | solution.py:518
  6.6 0.7 %iota_compare_fusion = pred[16,256]{1,0:T(8,128)(4,1)S(1)} fusion(s32[16]{0:T(128)} %lengths.1), kind=kLoop, calls=%fused_computation.2 | loop fusion | flops 4096 | bytes 4160 | tf_op jit(solution)/shard_map/eq | solution.py:22
  7.3 0.7 %reshape.52.gain = f32[1,1440]{1,0:T(1,128)S(1)} reshape(f32[1440]{0:T(1024)} %param.23) | data formatting | bytes 11520 | tf_op jit(solution)/shard_map/reshape | solution.py:506
  8.0 0.7 %copy.16.sink = f32[16,1]{1,0:T(8,128)S(1)} copy(f32[16,1]{0,1:T(1,128)} %bitcast.17) | data formatting | bytes 128 | tf_op jit(solution)/shard_map/reshape | solution.py:505
  8.8 0.8 %copy.17.expert_ids = s32[16,4]{1,0:T(8,128)S(1)} copy(s32[16,4]{0,1:T(4,128)} %param.25) | data formatting | bytes 512 | tf_op args[11]
  9.5 0.1 mul.25
  9.6 0.1 mul.26
  9.7 0.8 %broadcast_in_dim.23 = bf16[16,2,4,64]{3,2,1,0:T(4,128)(2,1)S(1)} reshape(bf16[16,2,256]{2,1,0:T(2,128)(2,1)} %param.16) | data formatting | bytes 32768 | tf_op jit(solution)/shard_map/jit(_where)/broadcast_in_dim | solution.py:21
  10.5 0.9 %mul.22 = bf16[16,4,4,64]{3,2,1,0:T(4,128)(2,1)S(1)} reshape(bf16[16,1024]{1,0:T(8,128)(2,1)} %param.15) | data formatting | bytes 65536 | tf_op jit(solution)/shard_map/mul | solution.py:450
  11.4 0.1 mul.23
  11.5 0.2 mul.24
  11.7 0.0 copy-start
  11.7 0.0 copy-start.1
  11.8 0.0 copy-start.2
  11.8 0.0 copy-start.3
  11.8 0.0 copy-start.4
  11.8 0.0 copy-start.5
  11.8 4.4 %broadcast_select_fusion = bf16[16,2,4,64,256]{4,3,2,1,0:T(8,128)(2,1)} fusion(bf16[16,2,4,64,256]{4,3,2,1,0:T(8,128)(2,1)} %param.17, pred[16,256]{1,0:T(8,128)(4,1)S(1)} %iota_compare_fusion, bf16[16,2,4,64]{3,2,1,0:T(4,128)(2,1)S(1)} %broadcast_in_dim.23), kind=kLoop, calls=%fused_computation | loop fusion | flops 2097152 | bytes 8409088 | tf_op jit(solution)/shard_map/jit(_where)/select_n | solution.py:21
  16.2 0.2 copy-done.1
  16.4 50.4 %shard_map.149 = (bf16[16,720]{1,0:T(8,128)(2,1)S(1)}, bf16[2,8,64,256]{3,2,1,0:T(8,128)(2,1)S(1)}) custom-call(s32[16]{0:T(128)S(1)} %copy-done.5, s32[2]{0:T(128)S(1)} %copy-done.4, s32[8,128]{1,0:T(8,128)S(1)} %broadcast_in_dim.21.meta, bf16[16,16,256]{2,1,0:T(8,128)(2,1)S(1)} %broadcast_multiply_fusion.queries, bf16[16,1440]{1,0:T(8,128)(2,1)S(1)} %copy-done.2, ...), custom_call_target="tpu_custom_call" | custom-call | tf_op jit(solution)/shard_map/pallas_call | solution.py:459
  66.9 0.7 %constant_dynamic-update-slice_fusion.1 = bf16[16,2,4,64,256]{4,3,2,1,0:T(8,128)(2,1)} fusion(bf16[16,2,4,64,256]{4,3,2,1,0:T(8,128)(2,1)} %broadcast_select_fusion, bf16[1,2,4,64,256]{4,3,2,1,0:T(8,128)(2,1)S(1)} %bitcast.16, s32[]{:T(128)S(6)} %select_n.11), kind=kLoop, calls=%fused_computation.7 | loop fusion | bytes 524292 | tf_op jit(solution)/shard_map/dynamic_update_slice | solution.py:517
  67.6 0.7 %constant_dynamic-update-slice_fusion = bf16[16,2,4,64,256]{4,3,2,1,0:T(8,128)(2,1)} fusion(bf16[16,2,4,64,256]{4,3,2,1,0:T(8,128)(2,1)} %constant_dynamic-update-slice_fusion.1, bf16[1,2,4,64,256]{4,3,2,1,0:T(8,128)(2,1)S(1)} %bitcast.15, s32[]{:T(128)S(6)} %select_n.12), kind=kLoop, calls=%fused_computation.6 | loop fusion | bytes 524292 | tf_op jit(solution)/shard_map/dynamic_update_slice | solution.py:517
  68.3 0.6 copy.21
  (10 shorter events, 0.1 us)
Async XLA Ops:
  11.7 4.4 %copy-start = (bf16[1024,1440]{0,1:T(8,128)(2,1)S(1)}, bf16[1024,1440]{0,1:T(8,128)(2,1)}, u32[]{:S(2)}) copy-start(bf16[1024,1440]{0,1:T(8,128)(2,1)} %param.22) | copy-start | bytes 8847364
  11.7 4.7 %copy-start.1 = (bf16[1,720,1440]{2,1,0:T(8,128)(2,1)S(1)}, bf16[1,720,1440]{2,1,0:T(8,128)(2,1)}, u32[]{:S(2)}) copy-start(bf16[1,720,1440]{2,1,0:T(8,128)(2,1)} %param.27) | copy-start | bytes 6220804
  11.8 4.7 %copy-start.2 = (bf16[16,1440]{1,0:T(8,128)(2,1)S(1)}, bf16[16,1440]{1,0:T(8,128)(2,1)}, u32[]{:S(2)}) copy-start(bf16[16,1440]{1,0:T(8,128)(2,1)} %residual.1) | copy-start | bytes 138244
  11.8 4.7 %copy-start.3 = (bf16[1440,8]{0,1:T(8,128)(2,1)S(1)}, bf16[1440,8]{0,1:T(8,128)(2,1)}, u32[]{:S(2)}) copy-start(bf16[1440,8]{0,1:T(8,128)(2,1)} %param.24) | copy-start | bytes 69124
  11.8 4.6 %copy-start.4 = (s32[2]{0:T(128)S(1)}, s32[2]{0:T(128)}, u32[]{:S(2)}) copy-start(s32[2]{0:T(128)} %slots.1) | copy-start | bytes 28
  11.8 4.6 %copy-start.5 = (s32[16]{0:T(128)S(1)}, s32[16]{0:T(128)}, u32[]{:S(2)}) copy-start(s32[16]{0:T(128)} %lengths.1) | copy-start | bytes 196

commit v2 on v1

--- a/solution.py
+++ b/solution.py
@@ -165,10 +165,11 @@
     n_tp,
     lengths,
     slots,
-    meta,
+    dests,
+    sink,
     queries,
+    new_kv,
     residual,
-    sink,
     gain,
     router,
     expert_ids,
@@ -178,9 +179,14 @@
     down_hbm,
     layer_out,
     incoming,
+    filled,
+    meta,
+    spread,
     cache,
     out_w,
     gate_up,
+    gate_w,
+    up_w,
     down_w,
     send1,
     recv1,
@@ -205,6 +211,7 @@
     stream_sems,
     y_sems,
     in_sem,
+    out_sem,
 ):
     ep = lax.axis_index("ep")
     tp = lax.axis_index("tp")
@@ -232,6 +239,13 @@
     for load in loads:
         load.start()
 
+    lane = lax.broadcasted_iota(jnp.int32, meta.shape, 1)
+    listing = jnp.zeros(meta.shape, jnp.int32)
+    for j in range(moves):
+        listing = jnp.where(lane == j, slots[j], listing)
+        listing = jnp.where(lane == moves + j, dests[j], listing)
+    meta[...] = listing
+
     barrier = pltpu.get_barrier_semaphore()
     for k in range(n_ep):
         for q in range(n_tp):
@@ -242,7 +256,6 @@
                     device_id={"ep": ahead(k), "tp": lax.rem(tp + q, n_tp)},
                     device_id_type=MESH,
                 )
-    pl.semaphore_wait(barrier, n_ep * n_tp - 1)
 
     def send(src, dst, sems, index, k, q=0):
         target = {"ep": ahead(k)} if k else {}
@@ -259,27 +272,56 @@
         copy.start()
         return copy
 
-    meta_copies = [send(meta, meta_all.at[k], meta_sems, (k,), k) for k in range(1, n_ep)]
-    meta_all[0] = meta[...]
+    fresh = [new_kv[:, i, :] for i in range(2)]
+    length = cache.shape[3]
+    row_of = lax.broadcasted_iota(jnp.int32, (rows, length), 0)
+    place_of = lax.broadcasted_iota(jnp.int32, (rows, length), 1)
+    place = lax.broadcasted_iota(jnp.int32, (kv * hd, length), 1)
+
+    def inserted(raw, i, r, last):
+        spot = jnp.where((row_of == r) & (place_of == last), 1.0, 0.0).astype(BF16)
+        column = lax.dot_general(
+            fresh[i], spot, (((0,), (0,)), ((), ())), preferred_element_type=F32
+        )
+        raw = raw.reshape(kv * hd, length).astype(F32)
+        return jnp.where(place == last, column, raw).astype(BF16)
 
     loads[0].wait()
     for j in range(moves):
         slot = slots[j]
-        for p in range(pieces):
-            send1[p, j] = cache[slot, p]
+        for i in range(2):
+            part = inserted(cache[slot, i * kv : (i + 1) * kv], i, slot, lengths[slot])
+            part = part.reshape(kv, hd, length)
+            for g in range(kv):
+                send1[i * kv + g, j] = part[g]
+    pl.semaphore_wait(barrier, n_ep * n_tp - 1)
+    meta_copies = [send(meta, meta_all.at[k], meta_sems, (k,), k) for k in range(1, n_ep)]
+    meta_all[0] = meta[...]
     one_copies = [
         send(send1.at[ahead(k)], recv1.at[k], one_sems, (k,), k) for k in range(1, n_ep)
     ]
     recv1[0] = send1[ep]
 
-    position_index = lax.broadcasted_iota(jnp.int32, (q_heads, cache.shape[3]), 1)
-    sink_part = sink[...]
+    position_index = lax.broadcasted_iota(jnp.int32, (q_heads, length), 1)
+    head_index = lax.broadcasted_iota(jnp.int32, (q_heads, 1), 0)
+    sink_part = jnp.zeros((q_heads, 1), F32)
+    for h in range(q_heads):
+        sink_part = jnp.where(head_index == h, sink[h], sink_part)
+    spread[...] = jnp.zeros(spread.shape, F32)
+    wide_queries = queries[...].astype(F32)
+    for h in range(q_heads):
+        g = h // group
+        spread[:, h, g * hd : (g + 1) * hd] = wide_queries[:, h * hd : (h + 1) * hd]
 
     def attend(r, carry):
-        keys = cache[r, 0:kv].reshape(kv * hd, cache.shape[3])
-        values = cache[r, kv : 2 * kv].reshape(kv * hd, cache.shape[3])
-        scores = jnp.dot(queries[r], keys, preferred_element_type=F32) * hd ** (-0.5)
-        visible = position_index <= lengths[r]
+        last = lengths[r]
+        keys = inserted(cache[r, 0:kv], 0, r, last)
+        values = inserted(cache[r, kv : 2 * kv], 1, r, last)
+        cache[r, 0:kv] = keys.reshape(kv, hd, length)
+        cache[r, kv : 2 * kv] = values.reshape(kv, hd, length)
+        asked = spread[r].astype(BF16)
+        scores = jnp.dot(asked, keys, preferred_element_type=F32) * hd ** (-0.5)
+        visible = position_index <= last
         peak = jnp.maximum(
             jnp.max(jnp.where(visible, scores, -1e30), axis=1, keepdims=True), sink_part
         )
@@ -292,6 +334,8 @@
         return carry
 
     lax.fori_loop(0, rows, attend, 0, unroll=4)
+    store = pltpu.make_async_copy(cache, filled, out_sem)
+    store.start()
     for h in range(0, q_heads, 2):
         g = h // group
         pair = [mixed[:, h + i, g * hd : (g + 1) * hd] for i in range(2)]
@@ -302,6 +346,8 @@
         heads[...], out_w[...], (((1,), (1,)), ((), ())), preferred_element_type=F32
     )
     part_copies = [send(partial, partial_in.at[q], part_sems, (q,), 0, q) for q in range(1, n_tp)]
+    loads[2].wait()
+    gate_w[...] = gate_up[:, 0, :]
     total = partial[...]
     for q in range(1, n_tp):
         part_copies[q - 1].wait()
@@ -312,6 +358,8 @@
     stream_copies = [
         send(streams.at[0], streams.at[k], stream_sems, (k,), k) for k in range(1, n_ep)
     ]
+
+    up_w[...] = gate_up[:, 1, :]
 
     for copy in meta_copies:
         copy.wait()
@@ -353,13 +401,13 @@
     two_copies = [send(send2.at[k], recv2.at[k], two_sems, (k,), k) for k in range(1, n_ep)]
     recv2[0] = send2[0]
 
+    gain_row = gain[...].reshape(1, width)
     known = streams[...].reshape(all_rows, width)
     wide = known.astype(F32)
     mean_square = jnp.sum(wide * wide, axis=1, keepdims=True) * (1.0 / width)
-    tokens = (wide * lax.rsqrt(mean_square + EPSILON) * gain[...]).astype(BF16)
-    loads[2].wait()
-    gate_part = jnp.dot(tokens, gate_up[:, 0, :], preferred_element_type=F32)
-    up_part = jnp.dot(tokens, gate_up[:, 1, :], preferred_element_type=F32)
+    tokens = (wide * lax.rsqrt(mean_square + EPSILON) * gain_row).astype(BF16)
+    gate_part = jnp.dot(tokens, gate_w[...], preferred_element_type=F32)
+    up_part = jnp.dot(tokens, up_w[...], preferred_element_type=F32)
     hidden[...] = ((up_part + 1.0) * gate_part * jax.nn.sigmoid(ALPHA * gate_part)).astype(BF16)
     moved = jnp.dot(move_to, hidden[...], preferred_element_type=F32).astype(BF16)
     loads[3].wait()
@@ -383,30 +431,38 @@
     brought = jnp.dot(move_to[0:rows], known, preferred_element_type=F32)
     new_stream = jnp.where(kept, own_stream[...], brought)
     mean_square = jnp.sum(new_stream * new_stream, axis=1, keepdims=True) * (1.0 / width)
-    normed = new_stream * lax.rsqrt(mean_square + EPSILON) * gain[...]
+    normed = new_stream * lax.rsqrt(mean_square + EPSILON) * gain_row
     logits = lax.dot_general(
+        router[...].astype(F32),
         normed,
-        router[...].astype(F32),
         (((1,), (1,)), ((), ())),
         precision=lax.Precision.HIGHEST,
         preferred_element_type=F32,
     )
-    expert_index = lax.broadcasted_iota(jnp.int32, logits.shape, 1)
+    expert_index = lax.broadcasted_iota(jnp.int32, logits.shape, 0)
     chosen = jnp.zeros(logits.shape, F32)
-    for t in range(expert_ids.shape[1]):
-        chosen = jnp.where(expert_index == expert_ids[:, t : t + 1], 1.0, chosen)
-    best = jnp.max(jnp.where(chosen > 0.5, logits, -1e30), axis=1, keepdims=True)
+    for t in range(expert_ids.shape[0]):
+        chosen = jnp.where(expert_index == expert_ids[t : t + 1, :], 1.0, chosen)
+    best = jnp.max(jnp.where(chosen > 0.5, logits, -1e30), axis=0, keepdims=True)
     raised = jnp.where(chosen > 0.5, jnp.exp(logits - best), 0.0)
-    gates = raised / jnp.sum(raised, axis=1, keepdims=True)
+    gates = raised / jnp.sum(raised, axis=0, keepdims=True)
+    slot_index = lax.broadcasted_iota(jnp.int32, (n_ep, n_ep), 1)
+    owner = lax.broadcasted_iota(jnp.int32, (n_ep, n_ep), 0)
+    order = jnp.where(wrap(ep - slot_index, n_ep) == owner, 1.0, 0.0)
+    by_slot = lax.dot_general(
+        gates,
+        order,
+        (((0,), (0,)), ((), ())),
+        precision=lax.Precision.HIGHEST,
+        preferred_element_type=F32,
+    )
     result = new_stream[:, 0:half]
     for c in range(1, n_tp):
         result = jnp.where(tp == c, new_stream[:, c * half : (c + 1) * half], result)
     for copy in y_copies:
         copy.wait()
     for k in range(n_ep):
-        gate = jnp.sum(
-            jnp.where(expert_index == behind(k), gates, 0.0), axis=1, keepdims=True
-        )
+        gate = by_slot[:, k : k + 1]
         summed = yrecv[0, k].astype(F32)
         for q in range(1, n_tp):
             summed = summed + yrecv[q, k].astype(F32)
@@ -418,6 +474,7 @@
     for k in range(n_ep):
         for j in range(moves):
             incoming[j, behind(k)] = recv2[k, j]
+    store.wait()
 
 
 def per_device(
@@ -442,32 +499,31 @@
     _, _, kv, hd, length = kv_cache.shape
     moves = move_slot.shape[0]
     q_heads = sink_logits.shape[0]
-    group = q_heads // kv
     hidden_units = down_weight.shape[1]
-    filled = insert_token(kv_cache, new_kv, cache_len)
-    pieces = filled.reshape(rows, 2 * kv, hd, length)
-    same = jnp.eye(kv, dtype=queries.dtype).reshape(1, kv, 1, kv, 1)
-    spread = (queries.reshape(rows, kv, group, 1, hd) * same).reshape(rows, q_heads, kv * hd)
-    listing = jnp.concatenate([move_slot, move_dest])
-    meta = jnp.broadcast_to(jnp.pad(listing, (0, 128 - 2 * moves)), (8, 128))
+    pieces = kv_cache.reshape(rows, 2 * kv, hd, length)
     piece = (moves, hd, length)
     half = width // n_tp
     smem = pl.BlockSpec(memory_space=pltpu.SMEM)
     vmem = pl.BlockSpec(memory_space=pltpu.VMEM)
     hbm = pl.BlockSpec(memory_space=pl.ANY)
     dma = pltpu.SemaphoreType.DMA
-    layer_out, incoming = pl.pallas_call(
+    layer_out, incoming, filled = pl.pallas_call(
         functools.partial(step_kernel, n_ep, n_tp),
         out_shape=(
             jax.ShapeDtypeStruct((rows, half), BF16),
             jax.ShapeDtypeStruct((moves, 2 * kv, hd, length), BF16),
+            jax.ShapeDtypeStruct(pieces.shape, BF16),
         ),
-        in_specs=[smem] * 2 + [vmem] * 7 + [hbm] * 4,
-        out_specs=(vmem, vmem),
+        in_specs=[smem] * 4 + [vmem] * 6 + [hbm] * 4,
+        out_specs=(vmem, vmem, hbm),
         scratch_shapes=[
+            pltpu.VMEM((8, 128), jnp.int32),
+            pltpu.VMEM((rows, q_heads, kv * hd), F32),
             pltpu.VMEM(pieces.shape, BF16),
             pltpu.VMEM((width, out_weight.shape[0]), BF16),
             pltpu.VMEM((width, 2, hidden_units), BF16),
+            pltpu.VMEM((width, hidden_units), BF16),
+            pltpu.VMEM((width, hidden_units), BF16),
             pltpu.VMEM((hidden_units, width), BF16),
             pltpu.VMEM((2 * kv,) + piece, BF16),
             pltpu.VMEM((n_ep,) + piece, BF16),
@@ -492,31 +548,32 @@
             dma((2, n_ep)),
             dma((2, n_tp, n_ep)),
             dma,
+            dma,
         ],
         compiler_params=pltpu.CompilerParams(
-            collective_id=0, has_side_effects=True, vmem_limit_bytes=48 * 1024 * 1024
+            collective_id=0, has_side_effects=True, vmem_limit_bytes=58 * 1024 * 1024
         ),
     )(
         cache_len,
         move_slot,
-        meta,
-        spread,
+        move_dest,
+        sink_logits,
+        queries,
+        new_kv,
         residual,
-        sink_logits.reshape(q_heads, 1),
-        norm_gain.reshape(1, width),
+        norm_gain,
         router_weight.T,
-        expert_ids,
+        expert_ids.T,
         pieces,
         out_weight.T,
         gate_up[0],
         down_weight[0],
     )
-    incoming = incoming.reshape((moves,) + kv_cache.shape[1:])
+    row_index = lax.broadcasted_iota(jnp.int32, (rows, 1, 1, 1), 0)
     cache_out = filled
     for j in range(moves):
-        cache_out = lax.dynamic_update_slice(
-            cache_out, incoming[j : j + 1], (move_slot[j], 0, 0, 0, 0)
-        )
+        cache_out = jnp.where(row_index == move_slot[j], incoming[j][None], cache_out)
+    cache_out = cache_out.reshape(kv_cache.shape)
     return layer_out, cache_out
 
 

time: 69.4 us -> 60.3 us (0.87)
  local copies, waits for them, and re-layouts: 8.06 us -> 2.99 us
  between operations: 4.62 us -> 0.66 us
    dynamic_update_slice x2 -> x0, local copies, waits for them, and re-layouts: 1.45 us -> none  [per_device(): lax.dynamic_update_slice(cache_out, incoming[j:j + 1], (move_slot[j], 0,...]
    reshape x2 -> x0, local copies, waits for them, and re-layouts: 1.43 us -> none  [the longest x1 0.73 us: per_device(): sink_logits.reshape(q_heads, 1)]
    mul x5 -> x0, local copies, waits for them, and re-layouts: 1.36 us -> none  [per_device(): queries.reshape(rows, kv, group, 1, hd) * same]
    unnamed x14 -> x3, local copies, waits for them, and re-layouts: 1.64 us -> 0.61 us
    select_n x1, other arithmetic: 4.37 us -> 5.23 us  [per_device(): jnp.where(row_index == move_slot[j], incoming[j][None], cache_out)]
    concatenate x1 -> x0, other arithmetic: 0.75 us -> none  [per_device(): listing = jnp.concatenate([move_slot, move_dest])]
where the time goes in v2:
time: 60.3 us; the launch traced here: 60 us
  Pallas kernels  49.9 us (83%)
  other arithmetic  6.53 us (11%)
  local copies, waits for them, and re-layouts  2.99 us (5%)
  between operations  0.66 us (1%)
    pallas_call x1, Pallas kernels, per_device(): pl.pallas_call(functools.partial(step_kernel, n_ep, n_tp), out_shape=(jax...  49.9 us
    select_n x1, other arithmetic, per_device(): jnp.where(row_index == move_slot[j], incoming[j][None], cache_out)  5.23 us
    slice x1, local copies, waits for them, and re-layouts, per_device(): move_slot[j]  1.31 us
    eq x1, other arithmetic, per_device(): row_index == move_slot[j]  1.3 us

profile of v2, /device:TPU:1, one launch (start us, length us, event | category | flops | bytes accessed | tf_op | source)
XLA Modules:
  0.0 60.0 jit_solution(7550166538146274886)
XLA Ops:
  0.6 1.3 %fusion = (s32[1]{0:T(128)}, s32[1]{0:T(128)}) fusion(s32[2]{0:T(128)} %slots.1), kind=kLoop, calls=%fused_computation.5 | loop fusion | bytes 16 | tf_op jit(solution)/shard_map/slice | solution.py:575
  1.9 1.3 %iota_compare_fusion = (pred[16]{0:T(512)(128)(4,1)S(1)}, pred[16]{0:T(512)(128)(4,1)S(1)}) fusion(s32[]{:T(128)} %bitcast.8, s32[]{:T(128)} %bitcast.6), kind=kLoop, calls=%fused_computation.3 | loop fusion | flops 32 | bytes 40 | tf_op jit(solution)/shard_map/eq | solution.py:575
  3.2 49.9 %shard_map.149 = (bf16[16,720]{1,0:T(8,128)(2,1)}, bf16[2,8,64,256]{3,2,1,0:T(8,128)(2,1)}, bf16[16,8,64,256]{3,2,1,0:T(8,128)(2,1)}) custom-call(s32[16]{0:T(128)} %lengths.1, s32[2]{0:T(128)} %slots.1, s32[2]{0:T(128)} %dests.1, f32[16]{0:T(128)} %sink.1, bf16[16,1024]{1,0:T(8,128)(2,1)} %queries.1, bf16[16,2,256]{2,1,0:T(2,128)(2,1)} %new_kv.1, ...), custom_call_target="tpu_custom_call" | custom-call | tf_op jit(solution)/shard_map/pallas_call | solution.py:510
  53.1 1.1 %slice_bitcast_fusion.1 = (bf16[8,64,256]{2,1,0:T(8,128)(2,1)S(1)}, bf16[8,64,256]{2,1,0:T(8,128)(2,1)S(1)}) fusion(bf16[2,8,64,256]{3,2,1,0:T(8,128)(2,1)} %get-tuple-element.6), kind=kLoop, calls=%fused_computation.2 | loop fusion | bytes 1048576 | tf_op jit(solution)/shard_map/jit(_where)/broadcast_in_dim | solution.py:575
  54.2 0.0 copy-start
  54.2 5.2 %select_select_fusion = bf16[16,8,64,256]{3,2,1,0:T(8,128)(2,1)} fusion(bf16[16,8,64,256]{3,2,1,0:T(8,128)(2,1)} %get-tuple-element.7, pred[16]{0:T(512)(128)(4,1)S(1)} %get-tuple-element.12, pred[16]{0:T(512)(128)(4,1)S(1)} %get-tuple-element.13, bf16[8,64,256]{2,1,0:T(8,128)(2,1)S(1)} %get-tuple-element.9, bf16[8,64,256]{2,1,0:T(8,128)(2,1)S(1)} %get-tuple-element.8), kind=kLoop, calls=%fused_computation | loop fusion | flops 4194304 | bytes 8912928 | tf_op jit(solution)/shard_map/jit(_where)/select_n | solution.py:575
  59.4 0.0 copy-done
  59.4 0.6 %copy.17 = bf16[16,720]{1,0:T(8,128)(2,1)} copy(bf16[16,720]{1,0:T(8,128)(2,1)S(1)} %copy-done) | data formatting | bytes 46080
Async XLA Ops:
  54.2 5.2 %copy-start = (bf16[16,720]{1,0:T(8,128)(2,1)S(1)}, bf16[16,720]{1,0:T(8,128)(2,1)}, u32[]{:S(2)}) copy-start(bf16[16,720]{1,0:T(8,128)(2,1)} %get-tuple-element.16) | copy-start | bytes 69124

commit v3 on v2

--- a/solution.py
+++ b/solution.py
@@ -475,6 +475,28 @@
         for j in range(moves):
             incoming[j, behind(k)] = recv2[k, j]
     store.wait()
+
+
+def place_kernel(slots, filled, incoming, placed, row_sems, move_sems):
+    rows, moves = filled.shape[0], incoming.shape[0]
+    arrivals = [
+        pltpu.make_async_copy(incoming.at[j], placed.at[slots[j]], move_sems.at[j])
+        for j in range(moves)
+    ]
+    stays = []
+    for r in range(rows):
+        stay = slots[0] != r
+        for j in range(1, moves):
+            stay = stay & (slots[j] != r)
+        stays.append((stay, pltpu.make_async_copy(filled.at[r], placed.at[r], row_sems.at[r])))
+    for copy in arrivals:
+        copy.start()
+    for stay, copy in stays:
+        pl.when(stay)(copy.start)
+    for copy in arrivals:
+        copy.wait()
+    for stay, copy in stays:
+        pl.when(stay)(copy.wait)
 
 
 def per_device(
@@ -569,10 +591,13 @@
         gate_up[0],
         down_weight[0],
     )
-    row_index = lax.broadcasted_iota(jnp.int32, (rows, 1, 1, 1), 0)
-    cache_out = filled
-    for j in range(moves):
-        cache_out = jnp.where(row_index == move_slot[j], incoming[j][None], cache_out)
+    cache_out = pl.pallas_call(
+        place_kernel,
+        out_shape=jax.ShapeDtypeStruct(pieces.shape, BF16),
+        in_specs=[smem, hbm, hbm],
+        out_specs=hbm,
+        scratch_shapes=[dma((rows,)), dma((moves,))],
+    )(move_slot, filled, incoming)
     cache_out = cache_out.reshape(kv_cache.shape)
     return layer_out, cache_out
 

time: 60.3 us -> 180 us (2.99)
  Pallas kernels: 49.9 us -> 179 us
  other arithmetic: 6.53 us -> 0 us
  local copies, waits for them, and re-layouts: 2.99 us -> 0.61 us
    pallas_call x0 -> x1, Pallas kernels: none -> 129 us  [per_device(): pl.pallas_call(place_kernel, out_shape=jax.ShapeDtypeStruct(pieces.shape,...]
    select_n x1 -> x0, other arithmetic: 5.23 us -> none  [per_device(): jnp.where(row_index == move_slot[j], incoming[j][None], cache_out)]
where the time goes in v3:
time: 180 us
  Pallas kernels  179 us (99%)
    pallas_call x1, Pallas kernels, per_device(): pl.pallas_call(place_kernel, out_shape=jax.ShapeDtypeStruct(pieces.shape,...  129 us
    pallas_call x1, Pallas kernels, per_device(): pl.pallas_call(functools.partial(step_kernel, n_ep, n_tp), out_shape=(jax...  49.8 us

profile of v3, /device:TPU:1, one launch (start us, length us, event | category | flops | bytes accessed | tf_op | source)
XLA Modules:
  0.0 180.2 jit_solution(15514822131692035455)
XLA Ops:
  0.6 49.8 %shard_map.149 = (bf16[16,720]{1,0:T(8,128)(2,1)}, bf16[2,8,64,256]{3,2,1,0:T(8,128)(2,1)}, bf16[16,8,64,256]{3,2,1,0:T(8,128)(2,1)}) custom-call(s32[16]{0:T(128)} %lengths.1, s32[2]{0:T(128)} %slots.3, s32[2]{0:T(128)} %dests.1, f32[16]{0:T(128)} %sink.1, bf16[16,1024]{1,0:T(8,128)(2,1)} %queries.1, bf16[16,2,256]{2,1,0:T(2,128)(2,1)} %new_kv.1, ...), custom_call_target="tpu_custom_call" | custom-call | tf_op jit(solution)/shard_map/pallas_call | solution.py:532
  50.5 0.0 copy-start
  50.5 129.1 %shard_map.150 = bf16[16,8,64,256]{3,2,1,0:T(8,128)(2,1)} custom-call(s32[2]{0:T(128)} %slots.3, bf16[16,8,64,256]{3,2,1,0:T(8,128)(2,1)} %get-tuple-element.6.filled, bf16[2,8,64,256]{3,2,1,0:T(8,128)(2,1)} %get-tuple-element.7.incoming), custom_call_target="tpu_custom_call" | custom-call | tf_op jit(solution)/shard_map/pallas_call | solution.py:594
  179.6 0.0 copy-done
  179.6 0.6 copy.17
Async XLA Ops:
  50.5 129.1 %copy-start = (bf16[16,720]{1,0:T(8,128)(2,1)S(1)}, bf16[16,720]{1,0:T(8,128)(2,1)}, u32[]{:S(2)}) copy-start(bf16[16,720]{1,0:T(8,128)(2,1)} %get-tuple-element.10) | copy-start | bytes 69124
